TPU v7x, 32 devices: a whole 2x2x4 slice. The times are simulated.
32 devices in a mesh: row: 8 (over y, x, core), col: 4 (over z).
Axes of the slice: x: 2, y: 2, z: 4, core: 2. Of those that a mesh axis runs over, the one named last changes fastest.
Arguments:
- features: bfloat16 [16384, 1024], P(('row', 'col')), may hold values from 0 to 4, as said below
- coords: float32 [64, 16384], P(None, ('row', 'col')), may hold values from -1 to 1
Outputs:
- placed: float32 [64, 16384], P(None, ('row', 'col'))
- row_stress: float32 [16384], P(('row', 'col'))
- stress_norm: float32 [], replicated
Inputs may be any that keep to these rules, and one draw needn't show every extreme that they name: `features`: every molecule has at least one nonzero feature.
All inputs are finite; a program needn't handle non-finite values.
Results may differ from a plain program's by a relative error of at most 0.0003.
Values may be sent and summed in bfloat16 or wider, within the bound.
A program may use at most 192 MiB of HBM per device.

v0:
```python
import jax
import jax.numpy as jnp
from jax import lax
from jax.sharding import PartitionSpec as P

ITERS = 2
FLOOR = 0.25
EXACT = lax.Precision.HIGHEST


def from_root(block, axis, owner):
    block = jnp.where(lax.axis_index(axis) == owner, block, jnp.zeros_like(block))
    return lax.psum(block, axis)


def squares_of(values):
    return jnp.einsum("rf,rf->r", values, values, preferred_element_type=jnp.float32)


def tanimoto(left_rows, left_sq, right_rows):
    right_sq = squares_of(right_rows)
    common = lax.dot_general(
        left_rows, right_rows, (((1,), (1,)), ((), ())), preferred_element_type=jnp.float32
    )
    return 1.0 - common / (left_sq[:, None] + right_sq[None, :] - common)


def guttman_terms(dissim, x_rows, x_cols):
    coord_dim, row_len = x_rows.shape
    block_len = min(512, row_len)
    block_count = row_len // block_len
    col_norms = jnp.sum(x_cols * x_cols, axis=0)
    dis_blocks = dissim.reshape(block_count, block_len, dissim.shape[1])
    x_blocks = jnp.moveaxis(x_rows.reshape(coord_dim, block_count, block_len), 1, 0)

    def one_block(inputs):
        dis_blk, x_blk = inputs
        blk_norms = jnp.sum(x_blk * x_blk, axis=0)
        inner = lax.dot_general(
            x_blk,
            x_cols,
            (((0,), (0,)), ((), ())),
            precision=EXACT,
            preferred_element_type=jnp.float32,
        )
        distance = jnp.sqrt(
            jnp.maximum(blk_norms[:, None] + col_norms[None, :] - 2.0 * inner, FLOOR * FLOOR)
        )
        ratios = dis_blk / distance
        pulled = lax.dot_general(
            x_cols,
            ratios,
            (((1,), (1,)), ((), ())),
            precision=EXACT,
            preferred_element_type=jnp.float32,
        )
        pull_terms = x_blk * jnp.sum(ratios, axis=1)[None, :] - pulled
        stress = jnp.sum(jnp.square(dis_blk - distance), axis=1)
        return (pull_terms, stress)

    pull_terms, stress = lax.map(one_block, (dis_blocks, x_blocks))
    return (jnp.moveaxis(pull_terms, 0, 1).reshape(coord_dim, row_len), stress.reshape(row_len))


def on_device(features, coords):
    rows_n = lax.axis_size("row")
    cols_n = lax.axis_size("col")
    row_at = lax.axis_index("row")
    col_at = lax.axis_index("col")
    ratio_k = rows_n // cols_n
    share_len = coords.shape[1]
    row_len = share_len * cols_n
    molecules = row_len * rows_n
    feature_rows = lax.all_gather(features, "col", axis=0, tiled=True)
    rows_sq = squares_of(feature_rows)
    pieces = []
    for offset in range(ratio_k):
        feature_cols = from_root(feature_rows, "row", col_at * ratio_k + offset)
        pieces.append(tanimoto(feature_rows, rows_sq, feature_cols))
    dissim = jnp.concatenate(pieces, axis=1)
    dissim_sq = jnp.sum(dissim * dissim)
    current = coords
    row_stress = jnp.zeros((share_len,), jnp.float32)
    for sweep in range(ITERS):
        everything = lax.all_gather(current, ("row", "col"), axis=1, tiled=True)
        x_rows = lax.dynamic_slice_in_dim(everything, row_at * row_len, row_len, 1)
        x_cols = lax.dynamic_slice_in_dim(
            everything, col_at * row_len * ratio_k, row_len * ratio_k, 1
        )
        pull_terms, stress = guttman_terms(dissim, x_rows, x_cols)
        new_share, stress_share = (
            lax.psum_scatter(pull_terms, "col", scatter_dimension=1, tiled=True),
            lax.psum_scatter(stress, "col", scatter_dimension=0, tiled=True),
        )
        current = new_share / molecules
        row_stress = stress_share / molecules
    local_stress = jnp.sum(row_stress)
    stress_total, dissim_total = lax.psum((local_stress, dissim_sq), ("row", "col"))
    stress_norm = molecules * stress_total / dissim_total
    return (current, row_stress, stress_norm)


def solution(mesh):
    return jax.shard_map(
        on_device,
        mesh=mesh,
        in_specs=(P(("row", "col"), None), P(None, ("row", "col"))),
        out_specs=(P(None, ("row", "col")), P(("row", "col")), P()),
        check_vma=False,
    )
```

profile of v0, /device:TPU:0, one launch (start us, length us, event | category | flops | bytes accessed | tf_op | source)
XLA Modules:
  0.0 698.3 jit_solution(13126097829784607838)
XLA Ops:
  8.7 84.4 %all-gather.6.cloned.1.call-done = bf16[2048,1024]{1,0:T(8,128)(2,1)} async-done(((bf16[512,1024]{1,0:T(8,128)(2,1)}), bf16[2048,1024]{1,0:T(8,128)(2,1)}) %all-gather.6.cloned.1.call-update) | async-done | bytes 4194320 | tf_op jit(solution)/shard_map/all_gather | solution.py:74
  102.2 54.3 %all-gather.4.cloned.1.call-done = f32[64,16384]{1,0:T(8,128)} async-done(((f32[64,512]{1,0:T(8,128)}), f32[64,16384]{1,0:T(8,128)}) %all-gather.4.cloned.1.call-update) | async-done | bytes 4194320 | tf_op jit(solution)/shard_map/all_gather | solution.py:85
  159.3 126.3 %all-reduce.5.cloned.1.call-done = (bf16[2048,1024]{1,0:T(8,128)(2,1)}, bf16[2048,1024]{1,0:T(8,128)(2,1)}) async-done(((bf16[2048,1024]{1,0:T(8,128)(2,1)}, bf16[2048,1024]{1,0:T(8,128)(2,1)}), (bf16[2048,1024]{1,0:T(8,128)(2,1)}, bf16[2048,1024]{1,0:T(8,128)(2,1)})) %all-reduce.5.cloned.1.call-update) | async-done | bytes 8388624 | tf_op jit(solution)/shard_map/psum | solution.py:13
  290.9 11.4 %fusion.9 = f32[2048,2048]{0,1:T(8,128)S(1)} fusion(bf16[2048,1024]{1,0:T(8,128)(2,1)} %get-tuple-element.146, bf16[2048,1024]{1,0:T(8,128)(2,1)S(1)} %copy-done, f32[2048]{0:T(1024)S(1)} %get-tuple-element.161, f32[2048]{0:T(1024)S(1)} %fusion.13), kind=kOutput, calls=%fused_computation.25 | convolution fusion | flops 8606711808 | bytes 25182208 | tf_op jit(solution)/shard_map/dot_general | solution.py:22
  302.3 14.4 %fusion.10 = f32[2048,2048]{0,1:T(8,128)} fusion(bf16[2048,1024]{1,0:T(8,128)(2,1)} %get-tuple-element.145, bf16[2048,1024]{1,0:T(8,128)(2,1)S(1)} %copy-done, f32[2048]{0:T(1024)S(1)} %get-tuple-element.160, f32[2048]{0:T(1024)S(1)} %fusion.13), kind=kOutput, calls=%fused_computation.26 | convolution fusion | flops 8606711808 | bytes 25182208 | tf_op jit(solution)/shard_map/dot_general | solution.py:22
  316.7 20.2 %multiply_reduce_fusion.2 = (f32[]{:T(128)}, f32[2048,4096]{0,1:T(8,128)}) fusion(f32[2048,2048]{0,1:T(8,128)} %fusion.10, f32[2048,2048]{0,1:T(8,128)S(1)} %fusion.9), kind=kLoop, calls=%fused_computation.22 | loop fusion | flops 25165824 | bytes 67108864 | tf_op jit(solution)/shard_map/reduce_sum | solution.py:81
  336.9 31.1 %copy.33 = f32[2048,4096]{1,0:T(8,128)} copy(f32[2048,4096]{0,1:T(8,128)} %get-tuple-element.157) | data formatting | bytes 67108864 | tf_op jit(solution)/shard_map/while | solution.py:61
  368.0 78.5 %while.22 = (s32[]{:T(128)}, f32[4,64,512]{2,1,0:T(8,128)S(1)}, f32[4,64,512]{2,0,1:T(4,128)S(1)}, f32[4,512,4096]{2,1,0:T(8,128)}, f32[4096]{0:T(1024)S(1)}, /*index=5*/f32[64,4096]{1,0:T(8,128)S(1)}, s32[]{:T(128)}) while((s32[]{:T(128)}, f32[4,64,512]{2,1,0:T(8,128)S(1)}, f32[4,64,512]{2,0,1:T(4,128)S(1)}, f32[4,512,4096]{2,1,0:T(8,128)}, ...), condition=%wide.region_6.7_spmd, body=%wide.region_3.6_spmd.sunk | while | flops 3233938432 | bytes 28074072 | solution.py:61
  368.4 11.1 %fusion.37 = (f32[512]{0:T(512)S(1)}, f32[512,4096]{1,0:T(8,128)S(1)}) fusion(f32[64,4096]{1,0:T(8,128)S(1)} %get-tuple-element.271, f32[1,64,512]{2,0,1:T(1,128)S(1)} %constant_dynamic-slice_fusion.10, f32[4096]{0:T(1024)S(1)} %get-tuple-element.270, f32[512]{0:T(512)S(1)} %multiply_reduce_fusion.7, f32[4,512,4096]{2,1,0:T(8,128)} %get-tuple-element.269, ...), kind=kOutput, calls=%fused_computation.45.clone.1 | convolution fusion | flops 1623195136 | bytes 17977348 | tf_op jit(solution)/shard_map/while/body/eval_jaxpr/dot_general | solution.py:39
  388.0 11.1 %fusion.37 = (f32[512]{0:T(512)S(1)}, f32[512,4096]{1,0:T(8,128)S(1)}) fusion(f32[64,4096]{1,0:T(8,128)S(1)} %get-tuple-element.271, f32[1,64,512]{2,0,1:T(1,128)S(1)} %constant_dynamic-slice_fusion.10, f32[4096]{0:T(1024)S(1)} %get-tuple-element.270, f32[512]{0:T(512)S(1)} %multiply_reduce_fusion.7, f32[4,512,4096]{2,1,0:T(8,128)} %get-tuple-element.269, ...), kind=kOutput, calls=%fused_computation.45.clone.1 | convolution fusion | flops 1623195136 | bytes 17977348 | tf_op jit(solution)/shard_map/while/body/eval_jaxpr/dot_general | solution.py:39
  407.5 11.1 %fusion.37 = (f32[512]{0:T(512)S(1)}, f32[512,4096]{1,0:T(8,128)S(1)}) fusion(f32[64,4096]{1,0:T(8,128)S(1)} %get-tuple-element.271, f32[1,64,512]{2,0,1:T(1,128)S(1)} %constant_dynamic-slice_fusion.10, f32[4096]{0:T(1024)S(1)} %get-tuple-element.270, f32[512]{0:T(512)S(1)} %multiply_reduce_fusion.7, f32[4,512,4096]{2,1,0:T(8,128)} %get-tuple-element.269, ...), kind=kOutput, calls=%fused_computation.45.clone.1 | convolution fusion | flops 1623195136 | bytes 17977348 | tf_op jit(solution)/shard_map/while/body/eval_jaxpr/dot_general | solution.py:39
  427.1 11.1 %fusion.37 = (f32[512]{0:T(512)S(1)}, f32[512,4096]{1,0:T(8,128)S(1)}) fusion(f32[64,4096]{1,0:T(8,128)S(1)} %get-tuple-element.271, f32[1,64,512]{2,0,1:T(1,128)S(1)} %constant_dynamic-slice_fusion.10, f32[4096]{0:T(1024)S(1)} %get-tuple-element.270, f32[512]{0:T(512)S(1)} %multiply_reduce_fusion.7, f32[4,512,4096]{2,1,0:T(8,128)} %get-tuple-element.269, ...), kind=kOutput, calls=%fused_computation.45.clone.1 | convolution fusion | flops 1623195136 | bytes 17977348 | tf_op jit(solution)/shard_map/while/body/eval_jaxpr/dot_general | solution.py:39
  447.4 21.9 %reduce-scatter.3.cloned.1.call-done = f32[64,512]{1,0:T(8,128)} async-done(((f32[64,2048]{1,0:T(8,128)}), f32[64,512]{1,0:T(8,128)}) %reduce-scatter.3.cloned.1.call-update) | async-done | bytes 131088 | tf_op jit(solution)/shard_map/reduce_scatter | solution.py:92
  471.0 62.4 %all-gather.8.cloned.1.call-done = f32[64,16384]{1,0:T(8,128)} async-done(((f32[64,512]{1,0:T(8,128)}), f32[64,16384]{1,0:T(8,128)}) %all-gather.8.cloned.1.call-update) | async-done | bytes 4194320 | tf_op jit(solution)/shard_map/all_gather | solution.py:85
  536.3 98.9 %while.23 = (s32[]{:T(128)}, f32[4,64,512]{2,1,0:T(8,128)S(1)}, f32[4,512]{1,0:T(4,128)S(1)}, f32[4,64,512]{2,0,1:T(4,128)S(1)}, f32[4,512,4096]{2,1,0:T(8,128)}...) while((s32[]{:T(128)}, f32[4,64,512]{2,1,0:T(8,128)S(1)}, ...), condition=%wide.region_13.14_spmd, body=%wide.region_9.13_spmd.sunk | while | flops 3242326528 | bytes 36469864 | solution.py:61
  536.7 13.9 %fusion.41 = (f32[512]{0:T(512)S(1)}, f32[512]{0:T(512)S(1)}, f32[512,4096]{1,0:T(8,128)S(1)}) fusion(f32[4,512,4096]{2,1,0:T(8,128)} %get-tuple-element.295, s32[]{:T(128)} %get-tuple-element.282, f32[64,4096]{1,0:T(8,128)S(1)} %get-tuple-element.297, f32[1,64,512]{2,0,1:T(1,128)S(1)} %constant_dynamic-slice_fusion.11, ...), kind=kOutput, calls=%fused_computation.11.clone.1 | convolution fusion | flops 1629486080 | bytes 17979396 | tf_op jit(solution)/shard_map/while/body/eval_jaxpr/dot_general | solution.py:39
  550.6 10.5 %fusion.42 = f32[4,64,512]{2,1,0:T(8,128)S(1)} fusion(f32[4,64,512]{2,1,0:T(8,128)S(1)} %get-tuple-element.283, s32[]{:T(128)} %get-tuple-element.282, f32[64,4096]{1,0:T(8,128)S(1)} %get-tuple-element.297, f32[1,64,512]{2,0,1:T(1,128)S(1)} %constant_dynamic-slice_fusion.11, f32[512]{0:T(512)S(1)} %get-tuple-element.249, ...), kind=kOutput, calls=%fused_computation.16.clone.1 | convolution fusion | flops 1612775424 | bytes 18091008 | tf_op jit(solution)/shard_map/while/body/eval_jaxpr/dot_general | solution.py:50
  561.4 13.9 %fusion.41 = (f32[512]{0:T(512)S(1)}, f32[512]{0:T(512)S(1)}, f32[512,4096]{1,0:T(8,128)S(1)}) fusion(f32[4,512,4096]{2,1,0:T(8,128)} %get-tuple-element.295, s32[]{:T(128)} %get-tuple-element.282, f32[64,4096]{1,0:T(8,128)S(1)} %get-tuple-element.297, f32[1,64,512]{2,0,1:T(1,128)S(1)} %constant_dynamic-slice_fusion.11, ...), kind=kOutput, calls=%fused_computation.11.clone.1 | convolution fusion | flops 1629486080 | bytes 17979396 | tf_op jit(solution)/shard_map/while/body/eval_jaxpr/dot_general | solution.py:39
  586.0 13.9 %fusion.41 = (f32[512]{0:T(512)S(1)}, f32[512]{0:T(512)S(1)}, f32[512,4096]{1,0:T(8,128)S(1)}) fusion(f32[4,512,4096]{2,1,0:T(8,128)} %get-tuple-element.295, s32[]{:T(128)} %get-tuple-element.282, f32[64,4096]{1,0:T(8,128)S(1)} %get-tuple-element.297, f32[1,64,512]{2,0,1:T(1,128)S(1)} %constant_dynamic-slice_fusion.11, ...), kind=kOutput, calls=%fused_computation.11.clone.1 | convolution fusion | flops 1629486080 | bytes 17979396 | tf_op jit(solution)/shard_map/while/body/eval_jaxpr/dot_general | solution.py:39
  599.9 10.5 %fusion.42 = f32[4,64,512]{2,1,0:T(8,128)S(1)} fusion(f32[4,64,512]{2,1,0:T(8,128)S(1)} %get-tuple-element.283, s32[]{:T(128)} %get-tuple-element.282, f32[64,4096]{1,0:T(8,128)S(1)} %get-tuple-element.297, f32[1,64,512]{2,0,1:T(1,128)S(1)} %constant_dynamic-slice_fusion.11, f32[512]{0:T(512)S(1)} %get-tuple-element.249, ...), kind=kOutput, calls=%fused_computation.16.clone.1 | convolution fusion | flops 1612775424 | bytes 18091008 | tf_op jit(solution)/shard_map/while/body/eval_jaxpr/dot_general | solution.py:50
  610.7 13.9 %fusion.41 = (f32[512]{0:T(512)S(1)}, f32[512]{0:T(512)S(1)}, f32[512,4096]{1,0:T(8,128)S(1)}) fusion(f32[4,512,4096]{2,1,0:T(8,128)} %get-tuple-element.295, s32[]{:T(128)} %get-tuple-element.282, f32[64,4096]{1,0:T(8,128)S(1)} %get-tuple-element.297, f32[1,64,512]{2,0,1:T(1,128)S(1)} %constant_dynamic-slice_fusion.11, ...), kind=kOutput, calls=%fused_computation.11.clone.1 | convolution fusion | flops 1629486080 | bytes 17979396 | tf_op jit(solution)/shard_map/while/body/eval_jaxpr/dot_general | solution.py:39
  624.6 10.5 %fusion.42 = f32[4,64,512]{2,1,0:T(8,128)S(1)} fusion(f32[4,64,512]{2,1,0:T(8,128)S(1)} %get-tuple-element.283, s32[]{:T(128)} %get-tuple-element.282, f32[64,4096]{1,0:T(8,128)S(1)} %get-tuple-element.297, f32[1,64,512]{2,0,1:T(1,128)S(1)} %constant_dynamic-slice_fusion.11, f32[512]{0:T(512)S(1)} %get-tuple-element.249, ...), kind=kOutput, calls=%fused_computation.16.clone.1 | convolution fusion | flops 1612775424 | bytes 18091008 | tf_op jit(solution)/shard_map/while/body/eval_jaxpr/dot_general | solution.py:50
  637.3 10.5 %all-reduce = f32[2048]{0:T(1024)S(1)} all-reduce(f32[2048]{0:T(1024)S(1)} %bitcast.124), channel_id=4, replica_groups=mesh['row'=8,'col'=4] {'col'}, use_global_device_ids=true, to_apply=%region_15.16.clone | all-reduce | flops 2048 | bytes 16384
  649.1 38.3 %all-reduce.1 = (f32[]{:T(128)}, f32[]{:T(128)}) all-reduce(f32[]{:T(128)} %get-tuple-element.147, f32[]{:T(128)} %get-tuple-element.156), channel_id=1, replica_groups=mesh['row'=8,'col'=4] {'row','col'}, use_global_device_ids=true, to_apply=%region_17.18 | all-reduce | flops 2 | bytes 16 | tf_op jit(solution)/shard_map/psum | solution.py:98
  (61 shorter events, 73.2 us)
Async XLA Ops:
  7.2 85.9 %all-gather.6.cloned.1.call-start = ((), (), s32[]{:S(2)}) async-start(), calls=%async_computation.3 | async-start | bytes 5242880 | tf_op jit(solution)/shard_map/all_gather | solution.py:74
  7.9 148.6 %all-gather.4.cloned.1.call-start = ((), (), s32[]{:S(2)}) async-start(), calls=%async_computation.2 | async-start | bytes 4325376 | tf_op jit(solution)/shard_map/all_gather | solution.py:85
  8.6 276.9 %all-reduce.5.cloned.1.call-start = ((), (), s32[]{:S(2)}) async-start(), calls=%async_computation.7 | async-start | bytes 16777216 | tf_op jit(solution)/shard_map/psum | solution.py:13
  99.0 370.3 %reduce-scatter.3.cloned.1.call-start = ((), (), s32[]{:S(2)}) async-start(), calls=%async_computation.4 | async-start | bytes 655360 | tf_op jit(solution)/shard_map/reduce_scatter | solution.py:92
  285.5 5.3 copy-start
  447.4 86.0 %all-gather.8.cloned.1.call-start = ((), (), s32[]{:S(2)}) async-start(), calls=%async_computation.5 | async-start | bytes 4325376 | tf_op jit(solution)/shard_map/all_gather | solution.py:85
  470.9 217.8 %reduce-scatter.5.cloned.1.call-start = ((), (), s32[]{:S(2)}) async-start(), calls=%async_computation.6 | async-start | bytes 655360 | tf_op jit(solution)/shard_map/reduce_scatter | solution.py:92
  536.3 99.8 %copy-start.1 = (u32[32]{0:T(128)S(1)}, u32[32]{0:T(128)}, u32[]{:S(2)}) copy-start(u32[32]{0:T(128)} %constant.75) | copy-start | bytes 388
Sparse Core Ops, SparseCore 0:
  9.6 83.4 all-gather.5
  96.1 60.2 all-gather.3
  160.2 125.3 all-reduce.4
  447.5 21.7 reduce-scatter.2
  473.3 60.0 all-gather.7
  636.2 19.9 reduce-scatter.4
where the time goes:
time: 699 us; the launch traced here: 698 us
  waiting for transfers between devices  351 us (50%)
  matrix products  201 us (29%)
  blocking collectives  48.8 us (7%)
  other arithmetic  41.9 us (6%)
  local copies, waits for them, and re-layouts  37.5 us (5%)
  between operations  17.4 us (2%)
    psum x1, waiting for transfers between devices, from_root(): return lax.psum(block, axis)  126 us
    all_gather x2, waiting for transfers between devices, on_device(): everything = lax.all_gather(current, ('row', 'col'), axis=1, tiled=True)  117 us
    dot_general x8, matrix products, one_block(): lax.dot_general(x_blk, x_cols, (((0,), (0,)), ((), ())), precision=EXACT,...  100 us
    all_gather x1, waiting for transfers between devices, on_device(): feature_rows = lax.all_gather(features, 'col', axis=0, tiled=True)  84.4 us
    dot_general x8, matrix products, one_block(): lax.dot_general(x_cols, ratios, (((1,), (1,)), ((), ())), precision=EXACT...  74.9 us
    psum x1, blocking collectives, on_device(): lax.psum((local_stress, dissim_sq), ('row', 'col'))  38.3 us
    while x1, local copies, waits for them, and re-layouts, guttman_terms(): pull_terms, stress = lax.map(one_block, (dis_blocks, x_blocks))  31.1 us
    dot_general x2, matrix products, tanimoto(): lax.dot_general(left_rows, right_rows, (((1,), (1,)), ((), ())), preferre...  25.8 us
  transfers between devices with their start and end apart: 6, of which 5 were waited for; matrix products, arithmetic and copies ran while one was open for 2% of the time, Pallas kernels for 0%

commit v1 on v0

--- a/solution.py
+++ b/solution.py
@@ -71,7 +71,16 @@
     share_len = coords.shape[1]
     row_len = share_len * cols_n
     molecules = row_len * rows_n
-    feature_rows = lax.all_gather(features, "col", axis=0, tiled=True)
+    ways = lax.axis_size("col")
+    up = [(d, (d + 1) % ways) for d in range(ways)]
+    down = [(d, (d - 1) % ways) for d in range(ways)]
+    earlier, later = ([features], [features])
+    for _ in range(ways // 2):
+        earlier.append(lax.ppermute(earlier[-1], "col", up))
+    for _ in range((ways - 1) // 2):
+        later.append(lax.ppermute(later[-1], "col", down))
+    line = jnp.concatenate([*earlier[::-1], *later[1:]], axis=0)
+    feature_rows = jnp.roll(line, (lax.axis_index("col") - ways // 2) * features.shape[0], axis=0)
     rows_sq = squares_of(feature_rows)
     pieces = []
     for offset in range(ratio_k):

time: 699 us -> 647 us (0.926)
  waiting for transfers between devices: 351 us -> 276 us
  local copies, waits for them, and re-layouts: 37.5 us -> 44.9 us
    all_gather x1 -> x0, waiting for transfers between devices: 84.4 us -> none  [on_device(): feature_rows = lax.all_gather(features, 'col', axis=0, tiled=True)]
    ppermute x0 -> x3, waiting for transfers between devices: none -> 65.9 us  [the longest x2 49.6 us: on_device(): earlier.append(lax.ppermute(earlier[-1], 'col', up))]
    all_gather x2, waiting for transfers between devices: 117 us -> 60.2 us  [on_device(): everything = lax.all_gather(current, ('row', 'col'), axis=1, tiled=True)]
    unnamed x6 -> x19, local copies, waits for them, and re-layouts: 0.6 us -> 7.99 us
  transfers between devices with their start and end apart: 6 -> 8, of which waited for: 5 -> 6; matrix products, arithmetic and copies ran while one was open for 2% -> 14% of each run, Pallas kernels for 0% -> 0%
where the time goes in v1:
time: 647 us; the launch traced here: 641 us
  waiting for transfers between devices  276 us (43%)
  matrix products  204 us (32%)
  blocking collectives  48.9 us (8%)
  local copies, waits for them, and re-layouts  44.9 us (7%)
  other arithmetic  41.1 us (6%)
  between operations  18.8 us (3%)
  starting transfers between devices  7.11 us (1%)
    psum x1, waiting for transfers between devices, from_root(): return lax.psum(block, axis)  128 us
    dot_general x8, matrix products, one_block(): lax.dot_general(x_blk, x_cols, (((0,), (0,)), ((), ())), precision=EXACT,...  100 us
    dot_general x8, matrix products, one_block(): lax.dot_general(x_cols, ratios, (((1,), (1,)), ((), ())), precision=EXACT...  74.9 us
    all_gather x2, waiting for transfers between devices, on_device(): everything = lax.all_gather(current, ('row', 'col'), axis=1, tiled=True)  60.2 us
    ppermute x2, waiting for transfers between devices, on_device(): earlier.append(lax.ppermute(earlier[-1], 'col', up))  49.6 us
    psum x1, blocking collectives, on_device(): lax.psum((local_stress, dissim_sq), ('row', 'col'))  38.2 us
    while x1, local copies, waits for them, and re-layouts, guttman_terms(): pull_terms, stress = lax.map(one_block, (dis_blocks, x_blocks))  31.1 us
    dot_general x2, matrix products, tanimoto(): lax.dot_general(left_rows, right_rows, (((1,), (1,)), ((), ())), preferre...  28.3 us
  transfers between devices with their start and end apart: 8, of which 6 were waited for; matrix products, arithmetic and copies ran while one was open for 14% of the time, Pallas kernels for 0%

profile of v1, /device:TPU:0, one launch (start us, length us, event | category | flops | bytes accessed | tf_op | source)
XLA Modules:
  0.0 641.2 jit_solution(17934331471184371748)
XLA Ops:
  11.1 25.4 %collective-permute-done = bf16[512,1024]{1,0:T(8,128)(2,1)S(1)} collective-permute-done((bf16[512,1024]{1,0:T(8,128)(2,1)}, bf16[512,1024]{1,0:T(8,128)(2,1)S(1)}, u32[]{:S(2)}, u32[]{:S(2)}) %collective-permute-start) | collective-permute-done | bytes 1048608 | tf_op jit(solution)/shard_map/ppermute | solution.py:79
  40.4 24.2 %collective-permute-done.1 = bf16[512,1024]{1,0:T(8,128)(2,1)} collective-permute-done((bf16[512,1024]{1,0:T(8,128)(2,1)S(1)}, bf16[512,1024]{1,0:T(8,128)(2,1)}, u32[]{:S(2)}, u32[]{:S(2)}) %collective-permute-start.1) | collective-permute-done | bytes 1048608 | tf_op jit(solution)/shard_map/ppermute | solution.py:79
  67.2 16.4 %collective-permute-done.2 = bf16[512,1024]{1,0:T(8,128)(2,1)S(1)} collective-permute-done((bf16[512,1024]{1,0:T(8,128)(2,1)}, bf16[512,1024]{1,0:T(8,128)(2,1)S(1)}, u32[]{:S(2)}, u32[]{:S(2)}) %collective-permute-start.2) | collective-permute-done | bytes 1048608 | tf_op jit(solution)/shard_map/ppermute | solution.py:81
  97.2 127.6 %all-reduce.5.cloned.1.call-done = (bf16[2048,1024]{1,0:T(8,128)(2,1)}, bf16[2048,1024]{1,0:T(8,128)(2,1)}) async-done(((bf16[2048,1024]{1,0:T(8,128)(2,1)}, bf16[2048,1024]{1,0:T(8,128)(2,1)}), (bf16[2048,1024]{1,0:T(8,128)(2,1)}, bf16[2048,1024]{1,0:T(8,128)(2,1)})) %all-reduce.5.cloned.1.call-update) | async-done | bytes 8388624 | tf_op jit(solution)/shard_map/psum | solution.py:13
  230.1 13.9 %fusion.9 = f32[2048,2048]{0,1:T(8,128)S(1)} fusion(f32[2048]{0:T(1024)S(1)} %get-tuple-element.161, f32[2048]{0:T(1024)S(1)} %fusion.13, bf16[2048,1024]{1,0:T(8,128)(2,1)} %get-tuple-element.146, bf16[4096,1024]{1,0:T(8,128)(2,1)} %copy-done, s32[]{:T(128)S(6)} %select_n.37), kind=kOutput, calls=%fused_computation.25 | convolution fusion | flops 8606711808 | bytes 25182212 | tf_op jit(solution)/shard_map/dot_general | solution.py:22
  244.1 14.4 %fusion.10 = f32[2048,2048]{0,1:T(8,128)} fusion(f32[2048]{0:T(1024)S(1)} %get-tuple-element.160, f32[2048]{0:T(1024)S(1)} %fusion.13, bf16[2048,1024]{1,0:T(8,128)(2,1)} %get-tuple-element.145, bf16[4096,1024]{1,0:T(8,128)(2,1)S(1)} %bitcast.112, s32[]{:T(128)S(6)} %select_n.37), kind=kOutput, calls=%fused_computation.26 | convolution fusion | flops 8606711808 | bytes 25182212 | tf_op jit(solution)/shard_map/dot_general | solution.py:22
  258.5 20.3 %multiply_reduce_fusion.2 = (f32[]{:T(128)}, f32[2048,4096]{0,1:T(8,128)}) fusion(f32[2048,2048]{0,1:T(8,128)} %fusion.10, f32[2048,2048]{0,1:T(8,128)S(1)} %fusion.9), kind=kLoop, calls=%fused_computation.22 | loop fusion | flops 25165824 | bytes 67108864 | tf_op jit(solution)/shard_map/reduce_sum | solution.py:90
  278.8 31.1 %copy.33 = f32[2048,4096]{1,0:T(8,128)} copy(f32[2048,4096]{0,1:T(8,128)} %get-tuple-element.157) | data formatting | bytes 67108864 | tf_op jit(solution)/shard_map/while | solution.py:61
  312.7 78.4 %while.22 = (s32[]{:T(128)}, f32[4,64,512]{2,1,0:T(8,128)S(1)}, f32[4,64,512]{2,0,1:T(4,128)S(1)}, f32[4,512,4096]{2,1,0:T(8,128)}, f32[4096]{0:T(1024)S(1)}, /*index=5*/f32[64,4096]{1,0:T(8,128)S(1)}, s32[]{:T(128)}) while((s32[]{:T(128)}, f32[4,64,512]{2,1,0:T(8,128)S(1)}, f32[4,64,512]{2,0,1:T(4,128)S(1)}, f32[4,512,4096]{2,1,0:T(8,128)}, ...), condition=%wide.region_6.7_spmd, body=%wide.region_3.6_spmd.sunk | while | flops 3233938432 | bytes 28074072 | solution.py:61
  313.1 11.2 %fusion.39 = (f32[512]{0:T(512)S(1)}, f32[512,4096]{1,0:T(8,128)S(1)}) fusion(f32[64,4096]{1,0:T(8,128)S(1)} %get-tuple-element.271, f32[1,64,512]{2,0,1:T(1,128)S(1)} %constant_dynamic-slice_fusion.10, f32[4096]{0:T(1024)S(1)} %get-tuple-element.270, f32[512]{0:T(512)S(1)} %multiply_reduce_fusion.7, f32[4,512,4096]{2,1,0:T(8,128)} %get-tuple-element.269, ...), kind=kOutput, calls=%fused_computation.57.clone.1 | convolution fusion | flops 1623195136 | bytes 17977348 | tf_op jit(solution)/shard_map/while/body/eval_jaxpr/dot_general | solution.py:39
  332.6 11.1 %fusion.39 = (f32[512]{0:T(512)S(1)}, f32[512,4096]{1,0:T(8,128)S(1)}) fusion(f32[64,4096]{1,0:T(8,128)S(1)} %get-tuple-element.271, f32[1,64,512]{2,0,1:T(1,128)S(1)} %constant_dynamic-slice_fusion.10, f32[4096]{0:T(1024)S(1)} %get-tuple-element.270, f32[512]{0:T(512)S(1)} %multiply_reduce_fusion.7, f32[4,512,4096]{2,1,0:T(8,128)} %get-tuple-element.269, ...), kind=kOutput, calls=%fused_computation.57.clone.1 | convolution fusion | flops 1623195136 | bytes 17977348 | tf_op jit(solution)/shard_map/while/body/eval_jaxpr/dot_general | solution.py:39
  352.2 11.1 %fusion.39 = (f32[512]{0:T(512)S(1)}, f32[512,4096]{1,0:T(8,128)S(1)}) fusion(f32[64,4096]{1,0:T(8,128)S(1)} %get-tuple-element.271, f32[1,64,512]{2,0,1:T(1,128)S(1)} %constant_dynamic-slice_fusion.10, f32[4096]{0:T(1024)S(1)} %get-tuple-element.270, f32[512]{0:T(512)S(1)} %multiply_reduce_fusion.7, f32[4,512,4096]{2,1,0:T(8,128)} %get-tuple-element.269, ...), kind=kOutput, calls=%fused_computation.57.clone.1 | convolution fusion | flops 1623195136 | bytes 17977348 | tf_op jit(solution)/shard_map/while/body/eval_jaxpr/dot_general | solution.py:39
  371.8 11.1 %fusion.39 = (f32[512]{0:T(512)S(1)}, f32[512,4096]{1,0:T(8,128)S(1)}) fusion(f32[64,4096]{1,0:T(8,128)S(1)} %get-tuple-element.271, f32[1,64,512]{2,0,1:T(1,128)S(1)} %constant_dynamic-slice_fusion.10, f32[4096]{0:T(1024)S(1)} %get-tuple-element.270, f32[512]{0:T(512)S(1)} %multiply_reduce_fusion.7, f32[4,512,4096]{2,1,0:T(8,128)} %get-tuple-element.269, ...), kind=kOutput, calls=%fused_computation.57.clone.1 | convolution fusion | flops 1623195136 | bytes 17977348 | tf_op jit(solution)/shard_map/while/body/eval_jaxpr/dot_general | solution.py:39
  392.1 21.9 %reduce-scatter.3.cloned.1.call-done = f32[64,512]{1,0:T(8,128)} async-done(((f32[64,2048]{1,0:T(8,128)}), f32[64,512]{1,0:T(8,128)}) %reduce-scatter.3.cloned.1.call-update) | async-done | bytes 131088 | tf_op jit(solution)/shard_map/reduce_scatter | solution.py:101
  415.7 60.2 %all-gather.5.cloned.1.call-done = f32[64,16384]{1,0:T(8,128)} async-done(((f32[64,512]{1,0:T(8,128)}), f32[64,16384]{1,0:T(8,128)}) %all-gather.5.cloned.1.call-update) | async-done | bytes 4194320 | tf_op jit(solution)/shard_map/all_gather | solution.py:94
  478.7 98.8 %while.23 = (s32[]{:T(128)}, f32[4,64,512]{2,1,0:T(8,128)S(1)}, f32[4,512]{1,0:T(4,128)S(1)}, f32[4,64,512]{2,0,1:T(4,128)S(1)}, f32[4,512,4096]{2,1,0:T(8,128)}...) while((s32[]{:T(128)}, f32[4,64,512]{2,1,0:T(8,128)S(1)}, ...), condition=%wide.region_13.14_spmd, body=%wide.region_9.13_spmd.sunk | while | flops 3242326528 | bytes 36469864 | solution.py:61
  479.1 13.9 %fusion.43 = (f32[512]{0:T(512)S(1)}, f32[512]{0:T(512)S(1)}, f32[512,4096]{1,0:T(8,128)S(1)}) fusion(f32[4,512,4096]{2,1,0:T(8,128)} %get-tuple-element.295, s32[]{:T(128)} %get-tuple-element.282, f32[64,4096]{1,0:T(8,128)S(1)} %get-tuple-element.297, f32[1,64,512]{2,0,1:T(1,128)S(1)} %constant_dynamic-slice_fusion.11, ...), kind=kOutput, calls=%fused_computation.11.clone.1 | convolution fusion | flops 1629486080 | bytes 17979396 | tf_op jit(solution)/shard_map/while/body/eval_jaxpr/dot_general | solution.py:39
  493.0 10.5 %fusion.44 = f32[4,64,512]{2,1,0:T(8,128)S(1)} fusion(f32[4,64,512]{2,1,0:T(8,128)S(1)} %get-tuple-element.283, s32[]{:T(128)} %get-tuple-element.282, f32[64,4096]{1,0:T(8,128)S(1)} %get-tuple-element.297, f32[1,64,512]{2,0,1:T(1,128)S(1)} %constant_dynamic-slice_fusion.11, f32[512]{0:T(512)S(1)} %get-tuple-element.249, ...), kind=kOutput, calls=%fused_computation.16.clone.1 | convolution fusion | flops 1612775424 | bytes 18091008 | tf_op jit(solution)/shard_map/while/body/eval_jaxpr/dot_general | solution.py:50
  503.8 13.9 %fusion.43 = (f32[512]{0:T(512)S(1)}, f32[512]{0:T(512)S(1)}, f32[512,4096]{1,0:T(8,128)S(1)}) fusion(f32[4,512,4096]{2,1,0:T(8,128)} %get-tuple-element.295, s32[]{:T(128)} %get-tuple-element.282, f32[64,4096]{1,0:T(8,128)S(1)} %get-tuple-element.297, f32[1,64,512]{2,0,1:T(1,128)S(1)} %constant_dynamic-slice_fusion.11, ...), kind=kOutput, calls=%fused_computation.11.clone.1 | convolution fusion | flops 1629486080 | bytes 17979396 | tf_op jit(solution)/shard_map/while/body/eval_jaxpr/dot_general | solution.py:39
  528.4 13.9 %fusion.43 = (f32[512]{0:T(512)S(1)}, f32[512]{0:T(512)S(1)}, f32[512,4096]{1,0:T(8,128)S(1)}) fusion(f32[4,512,4096]{2,1,0:T(8,128)} %get-tuple-element.295, s32[]{:T(128)} %get-tuple-element.282, f32[64,4096]{1,0:T(8,128)S(1)} %get-tuple-element.297, f32[1,64,512]{2,0,1:T(1,128)S(1)} %constant_dynamic-slice_fusion.11, ...), kind=kOutput, calls=%fused_computation.11.clone.1 | convolution fusion | flops 1629486080 | bytes 17979396 | tf_op jit(solution)/shard_map/while/body/eval_jaxpr/dot_general | solution.py:39
  542.3 10.5 %fusion.44 = f32[4,64,512]{2,1,0:T(8,128)S(1)} fusion(f32[4,64,512]{2,1,0:T(8,128)S(1)} %get-tuple-element.283, s32[]{:T(128)} %get-tuple-element.282, f32[64,4096]{1,0:T(8,128)S(1)} %get-tuple-element.297, f32[1,64,512]{2,0,1:T(1,128)S(1)} %constant_dynamic-slice_fusion.11, f32[512]{0:T(512)S(1)} %get-tuple-element.249, ...), kind=kOutput, calls=%fused_computation.16.clone.1 | convolution fusion | flops 1612775424 | bytes 18091008 | tf_op jit(solution)/shard_map/while/body/eval_jaxpr/dot_general | solution.py:50
  553.1 13.9 %fusion.43 = (f32[512]{0:T(512)S(1)}, f32[512]{0:T(512)S(1)}, f32[512,4096]{1,0:T(8,128)S(1)}) fusion(f32[4,512,4096]{2,1,0:T(8,128)} %get-tuple-element.295, s32[]{:T(128)} %get-tuple-element.282, f32[64,4096]{1,0:T(8,128)S(1)} %get-tuple-element.297, f32[1,64,512]{2,0,1:T(1,128)S(1)} %constant_dynamic-slice_fusion.11, ...), kind=kOutput, calls=%fused_computation.11.clone.1 | convolution fusion | flops 1629486080 | bytes 17979396 | tf_op jit(solution)/shard_map/while/body/eval_jaxpr/dot_general | solution.py:39
  579.7 10.7 %all-reduce = f32[2048]{0:T(1024)S(1)} all-reduce(f32[2048]{0:T(1024)S(1)} %bitcast.120), channel_id=4, replica_groups=mesh['row'=8,'col'=4] {'col'}, use_global_device_ids=true, to_apply=%region_15.16.clone | all-reduce | flops 2048 | bytes 16384
  591.6 38.2 %all-reduce.1 = (f32[]{:T(128)}, f32[]{:T(128)}) all-reduce(f32[]{:T(128)} %get-tuple-element.147, f32[]{:T(128)} %get-tuple-element.156), channel_id=1, replica_groups=mesh['row'=8,'col'=4] {'row','col'}, use_global_device_ids=true, to_apply=%region_17.18 | all-reduce | flops 2 | bytes 16 | tf_op jit(solution)/shard_map/psum | solution.py:107
  (79 shorter events, 96.3 us)
Async XLA Ops:
  8.0 77.0 %copy-start.1 = (bf16[512,1024]{1,0:T(8,128)(2,1)S(1)}, bf16[512,1024]{1,0:T(8,128)(2,1)}, u32[]{:S(2)}) copy-start(bf16[512,1024]{1,0:T(8,128)(2,1)} %param.6) | copy-start | bytes 3145732
  8.0 216.8 %all-reduce.5.cloned.1.call-start = ((), (), s32[]{:S(2)}) async-start(), calls=%async_computation.6 | async-start | bytes 16777216 | tf_op jit(solution)/shard_map/psum | solution.py:13
  8.1 28.5 %collective-permute-start = (bf16[512,1024]{1,0:T(8,128)(2,1)}, bf16[512,1024]{1,0:T(8,128)(2,1)S(1)}, u32[]{:S(2)}, u32[]{:S(2)}) collective-permute-start(bf16[512,1024]{1,0:T(8,128)(2,1)} %param.6), channel_id=1, source_target_pairs={{0,1},{1,2},{2,3},{3,0},{4,5},{5,6},{6,7},{7,4},{8,9},{9,10},{10,1... | collective-permute-start | bytes 3145736 | tf_op jit(solution)/shard_map/ppermute | solution.py:79
  36.5 28.0 %collective-permute-start.1 = (bf16[512,1024]{1,0:T(8,128)(2,1)S(1)}, bf16[512,1024]{1,0:T(8,128)(2,1)}, u32[]{:S(2)}, u32[]{:S(2)}) collective-permute-start(bf16[512,1024]{1,0:T(8,128)(2,1)S(1)} %collective-permute-done), channel_id=1, source_target_pairs={{0,1},{1,2},{2,3},{3,0},{4,5},{5,6},{6,7},{7,4},{8,9},{9,10},{10,1... | collective-permute-start | bytes 3145736 | tf_op jit(solution)/shard_map/ppermute | solution.py:79
  36.5 47.0 %collective-permute-start.2 = (bf16[512,1024]{1,0:T(8,128)(2,1)}, bf16[512,1024]{1,0:T(8,128)(2,1)S(1)}, u32[]{:S(2)}, u32[]{:S(2)}) collective-permute-start(bf16[512,1024]{1,0:T(8,128)(2,1)} %param.6), channel_id=1, source_target_pairs={{0,3},{1,0},{2,1},{3,2},{4,7},{5,4},{6,5},{7,6},{8,11},{9,8},{10,9... | collective-permute-start | bytes 3145736 | tf_op jit(solution)/shard_map/ppermute | solution.py:81
  85.2 3.2 copy-start
  93.5 216.4 %all-gather.3.cloned.1.call-start = ((), (), s32[]{:S(2)}) async-start(), calls=%async_computation.2 | async-start | bytes 4325376 | tf_op jit(solution)/shard_map/all_gather | solution.py:94
  94.0 320.0 %reduce-scatter.3.cloned.1.call-start = ((), (), s32[]{:S(2)}) async-start(), calls=%async_computation.3 | async-start | bytes 655360 | tf_op jit(solution)/shard_map/reduce_scatter | solution.py:101
  224.8 19.3 %slice-start = ((s8[8388608]{0:T(1024)(128)(4,1)}), s8[4194304]{0:T(1024)(128)(4,1)S(1)}, s32[]{:S(2)}) async-start(s8[8388608]{0:T(1024)(128)(4,1)} %bitcast.111), calls=%async_computation.7 | async-start | bytes 8388608
  230.1 14.0 %slice-start.1 = ((s8[8388608]{0:T(1024)(128)(4,1)}), s8[4194304]{0:T(1024)(128)(4,1)S(1)}, s32[]{:S(2)}) async-start(s8[8388608]{0:T(1024)(128)(4,1)} %bitcast.111), calls=%async_computation.8 | async-start | bytes 8388608
  392.0 83.8 %all-gather.5.cloned.1.call-start = ((), (), s32[]{:S(2)}) async-start(), calls=%async_computation.4 | async-start | bytes 4325376 | tf_op jit(solution)/shard_map/all_gather | solution.py:94
  415.6 215.6 %reduce-scatter.5.cloned.1.call-start = ((), (), s32[]{:S(2)}) async-start(), calls=%async_computation.5 | async-start | bytes 655360 | tf_op jit(solution)/shard_map/reduce_scatter | solution.py:101
  478.7 99.7 %copy-start.2 = (u32[32]{0:T(128)S(1)}, u32[32]{0:T(128)}, u32[]{:S(2)}) copy-start(u32[32]{0:T(128)} %constant.99) | copy-start | bytes 388
Sparse Core Ops, SparseCore 0:
  93.6 131.1 all-reduce.4
  392.1 21.8 reduce-scatter.2
  578.5 20.1 reduce-scatter.4
Sparse Core Ops, SparseCore 1:
  97.5 77.9 all-gather.2
  415.7 60.1 all-gather.4
